TPU v7x, 512 devices: a whole 4x8x8 slice. The times are simulated.
512 devices in a mesh: shot: 16 (over x_lo, z), tile: 32 (over y, x_hi, core).
Axes of the slice: x: 4 (x_hi: 2, x_lo: 2; x = x_hi * 2 + x_lo), y: 8, z: 8, core: 2. Of those that a mesh axis runs over, the one named last changes fastest.
Arguments:
- latent: bfloat16 [96, 16, 64, 64], P('tile', 'shot'), may hold values from -6 to 6
- kernel: bfloat16 [27, 64, 64], replicated, may hold values from -0.15625 to 0.15625
- conv_bias: float32 [64], replicated, may hold values from -3 to 3
- head_weight: bfloat16 [64], replicated, may hold values from -0.75 to 0.75
- density: float32 [192, 32, 128], P('tile'), may hold values from 1 to 2.5
- wave_prev: float32 [16, 192, 32, 128], P('shot', 'tile'), may hold values from -6 to 6
- wave_now: float32 [16, 192, 32, 128], P('shot', 'tile'), may hold values from -6 to 6
- adjoint_next: float32 [16, 192, 32, 128], P('shot', 'tile'), may hold values from -6 to 6
- adjoint_after: float32 [16, 192, 32, 128], P('shot', 'tile'), may hold values from -6 to 6
- source_cell: int32 [16], P('shot'), may hold values from 0 to 786431
- wavelet: float32 [16, 3], P('shot'), may hold values from -24 to 24
- receiver_cells: int32 [16, 128], P('shot'), may hold values from 0 to 786431
- observed: float32 [16, 3, 128], P('shot'), may hold values from -6 to 6
Outputs:
- latent_grad: float32 [96, 16, 64, 64], P('tile', 'shot')
- kernel_grad: float32 [27, 64, 64], replicated
- head_grad: float32 [64], replicated
- bias_grad: float32 [64], replicated
All inputs are finite; a program needn't handle non-finite values.
Results may differ from a plain program's by a relative error of at most 0.0034.
The roundings to bfloat16 on the way count: a program that leaves them out, or rounds other values in their place, can miss the bound.
Values may be sent and summed in bfloat16 or wider, within the bound.
No kernel may reach another device: no remote copies, remote signals or barrier semaphores. Data moves between devices by JAX's collectives and lax.ppermute only.
A program may use at most 64 MiB of HBM per device.

v0:
```python
import jax
import jax.numpy as jnp
from jax import lax
from jax.sharding import PartitionSpec as P

courant = 0.005
speed_low = 1.5
speed_span = 3.0


def padded_2(cells, sides, width):
    for axis, dim in sides:
        count = lax.axis_size(axis)
        ends = count - 1
        head = lax.slice_in_dim(cells, 0, width, axis=dim)
        tail = lax.slice_in_dim(cells, cells.shape[dim] - width, cells.shape[dim], axis=dim)
        cells = jnp.concatenate(
            [
                lax.ppermute(tail, axis, [(i, (i + 1) % count) for i in range(ends)]),
                cells,
                lax.ppermute(head, axis, [((i + 1) % count, i) for i in range(ends)]),
            ],
            axis=dim,
        )
    return cells


def upsample(coarse):
    coarse_x, coarse_z, channels, coarse_y = coarse.shape
    spread = jnp.broadcast_to(
        coarse[:, None, :, None, :, :, None], (coarse_x, 2, coarse_z, 2, channels, coarse_y, 2)
    )
    return spread.reshape(coarse_x * 2, coarse_z * 2, channels, coarse_y * 2)


def fold_children(fine):
    fine_x, fine_z, channels, fine_y = fine.shape
    grouped = fine.reshape(fine_x // 2, 2, fine_z // 2, 2, channels, fine_y // 2, 2)
    return jnp.sum(grouped, axis=(1, 3, 6))


def shifted_stack(padded, start_x, start_z, starts_y, cells_x, cells_z, cells_y):
    return jnp.concatenate(
        [
            padded[
                start_x : start_x + cells_x,
                start_z : start_z + cells_z,
                :,
                start_y : start_y + cells_y,
            ]
            for start_y in starts_y
        ],
        axis=2,
    )


def convolve(padded, kernel):
    cells_x = padded.shape[0] - 2
    cells_z = padded.shape[1] - 2
    channels = padded.shape[2]
    cells_y = padded.shape[3] - 2
    tap_table = kernel.reshape(3, 3, 3, channels, channels)
    result = jnp.zeros((cells_x, cells_z, channels, cells_y), jnp.float32)
    for offset_x in range(3):
        for offset_z in range(3):
            stacked = shifted_stack(
                padded, offset_x, offset_z, (0, 1, 2), cells_x, cells_z, cells_y
            )
            matrix = jnp.transpose(tap_table[offset_x, offset_z], (1, 0, 2)).reshape(
                channels, 3 * channels
            )
            result = result + jnp.einsum(
                "ok,abky->aboy", matrix, stacked, preferred_element_type=jnp.float32
            )
    return result


def kernel_terms(padded, grad_low):
    cells_x, cells_z, channels, cells_y = grad_low.shape
    pieces = []
    for offset_x in range(3):
        for offset_z in range(3):
            stacked = shifted_stack(
                padded, offset_x, offset_z, (0, 1, 2), cells_x, cells_z, cells_y
            )
            product = jnp.einsum(
                "aboy,abky->ok", grad_low, stacked, preferred_element_type=jnp.float32
            )
            pieces.append(jnp.transpose(product.reshape(channels, 3, channels), (1, 0, 2)))
    return jnp.stack(pieces).reshape(27, channels, channels)


def transposed(grad_padded, kernel):
    cells_x = grad_padded.shape[0] - 2
    cells_z = grad_padded.shape[1] - 2
    channels = grad_padded.shape[2]
    cells_y = grad_padded.shape[3] - 2
    tap_table = kernel.reshape(3, 3, 3, channels, channels)
    result = jnp.zeros((cells_x, cells_z, channels, cells_y), jnp.float32)
    for offset_x in range(3):
        for offset_z in range(3):
            stacked = shifted_stack(
                grad_padded, 2 - offset_x, 2 - offset_z, (2, 1, 0), cells_x, cells_z, cells_y
            )
            matrix = tap_table[offset_x, offset_z].reshape(3 * channels, channels)
            result = result + jnp.einsum(
                "kc,abky->abcy", matrix, stacked, preferred_element_type=jnp.float32
            )
    return result


def neighbours(padded):
    return (
        padded[2:, 1:-1, 1:-1],
        padded[:-2, 1:-1, 1:-1],
        padded[1:-1, 2:, 1:-1],
        padded[1:-1, :-2, 1:-1],
        padded[1:-1, 1:-1, 2:],
        padded[1:-1, 1:-1, :-2],
    )


def face_weights(padded_buoyancy):
    centre = padded_buoyancy[1:-1, 1:-1, 1:-1]
    return tuple((0.5 * (centre + beside) for beside in neighbours(padded_buoyancy)))


def apply_faces(padded, faces):
    centre = padded[1:-1, 1:-1, 1:-1]
    result = jnp.zeros_like(centre)
    for weight, beside in zip(faces, neighbours(padded)):
        result = result + weight * (beside - centre)
    return result


def propagate(
    laplace,
    coefficient,
    previous,
    current,
    following,
    beyond,
    anchor,
    source_cell,
    wavelet,
    receiver_cells,
    observed,
):
    field_shape = previous.shape
    field_cells = previous.size
    source_local = source_cell[0] - anchor
    source_owned = jnp.logical_and(source_local >= 0, source_local < field_cells).astype(
        jnp.float32
    )
    source_spot = jnp.clip(source_local, 0, field_cells - 1)
    receiver_local = receiver_cells[0] - anchor
    receiver_owned = jnp.logical_and(receiver_local >= 0, receiver_local < field_cells).astype(
        jnp.float32
    )
    receiver_spot = jnp.clip(receiver_local, 0, field_cells - 1)
    count_steps = wavelet.shape[1]
    laplacians = []
    residuals = []
    for instant in range(count_steps):
        laplacian = laplace(current)
        laplacians.append(laplacian)
        advanced = 2.0 * current - previous + coefficient * laplacian
        advanced = (
            advanced.reshape(-1)
            .at[source_spot]
            .add(source_owned * wavelet[0, instant])
            .reshape(field_shape)
        )
        residuals.append(
            receiver_owned * (advanced.reshape(-1)[receiver_spot] - observed[0, instant])
        )
        previous, current = (current, advanced)
    laplacians.append(laplace(current))
    coef_grad = following * laplacians[count_steps]
    for instant in reversed(range(count_steps)):
        preceding = 2.0 * following - beyond + laplace(coefficient * following)
        preceding = (
            preceding.reshape(-1).at[receiver_spot].add(residuals[instant]).reshape(field_shape)
        )
        coef_grad = coef_grad + preceding * laplacians[instant]
        beyond, following = (following, preceding)
    return coef_grad


def per_device(
    latent,
    kernel,
    conv_bias,
    head_weight,
    density,
    wave_prev,
    wave_now,
    adjoint_next,
    adjoint_after,
    source_cell,
    wavelet,
    receiver_cells,
    observed,
):
    extended = padded_2(upsample(latent), (("shot", 1), ("tile", 0)), 1)
    padded = jnp.pad(extended, ((0, 0), (0, 0), (0, 0), (1, 1)))
    pre_act = convolve(padded, kernel) + conv_bias[None, None, :, None]
    hidden = jax.nn.silu(pre_act).astype(jnp.bfloat16)
    logit = jnp.einsum("abcy,c->aby", hidden, head_weight, preferred_element_type=jnp.float32)
    squash = jax.nn.sigmoid(logit)
    velocity = speed_low + speed_span * squash
    tile_speed = lax.all_gather(velocity, "shot", axis=1, tiled=True)
    tile_cells = tile_speed.size
    buoyancy = 1.0 / density
    coefficient = courant * tile_speed * tile_speed * density
    factor = 2.0 * courant * tile_speed * density
    buoyancy_edges = padded_2(buoyancy, (("tile", 0),), 1)
    faces = face_weights(jnp.pad(buoyancy_edges, ((0, 0), (1, 1), (1, 1))))

    def laplace(field):
        field_edges = padded_2(field, (("tile", 0),), 1)
        return apply_faces(jnp.pad(field_edges, ((0, 0), (1, 1), (1, 1))), faces)

    anchor = lax.axis_index("tile") * tile_cells
    coef_grad = propagate(
        laplace,
        coefficient,
        wave_prev[0],
        wave_now[0],
        adjoint_next[0],
        adjoint_after[0],
        anchor,
        source_cell,
        wavelet,
        receiver_cells,
        observed,
    )
    strip_grad = lax.psum_scatter(coef_grad * factor, "shot", scatter_dimension=1, tiled=True)
    logit_grad = strip_grad * speed_span * squash * (1.0 - squash)
    head_part = jnp.einsum(
        "abcy,aby->c", hidden.astype(jnp.float32), logit_grad, precision=lax.Precision.HIGHEST
    )
    gate = jax.nn.sigmoid(pre_act)
    pre_grad = (
        logit_grad[:, :, None, :]
        * head_weight.astype(jnp.float32)[None, None, :, None]
        * (gate * (1.0 + pre_act * (1.0 - gate)))
    )
    bias_part = jnp.sum(pre_grad, axis=(0, 1, 3))
    grad_low = pre_grad.astype(jnp.bfloat16)
    kernel_part = kernel_terms(padded, grad_low)
    grad_edges = padded_2(grad_low, (("shot", 1), ("tile", 0)), 1)
    grad_padded = jnp.pad(grad_edges, ((0, 0), (0, 0), (0, 0), (1, 1)))
    latent_grad = fold_children(transposed(grad_padded, kernel))
    kernel_grad, head_grad, bias_grad = lax.psum(
        (kernel_part, head_part, bias_part), ("shot", "tile")
    )
    return (latent_grad, kernel_grad, head_grad, bias_grad)


def solution(mesh):
    return jax.shard_map(
        per_device,
        mesh=mesh,
        in_specs=(
            P("tile", "shot", None, None),
            P(),
            P(),
            P(),
            P("tile", None, None),
            P("shot", "tile", None, None),
            P("shot", "tile", None, None),
            P("shot", "tile", None, None),
            P("shot", "tile", None, None),
            P("shot"),
            P("shot", None),
            P("shot", None),
            P("shot", None, None),
        ),
        out_specs=(P("tile", "shot", None, None), P(), P(), P()),
        check_vma=False,
    )
```

profile of v0, /device:TPU:1, one launch (start us, length us, event | category | flops | bytes accessed | tf_op | source)
XLA Modules:
  0.0 589.9 jit_solution(18035886360403443610)
XLA Ops:
  7.2 0.9 copy.175
  8.4 4.8 collective-permute-start.1
  13.2 1.3 collective-permute-start.2
  14.5 0.7 slice_bitcast_fusion.6
  15.3 5.2 collective-permute-start.5
  20.5 2.2 collective-permute-start.7
  23.5 0.9 fusion.250
  25.4 0.7 fusion.256
  26.8 2.4 collective-permute-start.3
  29.2 1.9 collective-permute-start.4
  31.4 5.0 collective-permute-done.4
  36.3 0.6 fusion.13
  36.9 1.0 fusion.245
  41.6 0.3 multiply_convert_fusion
  42.4 32.4 %all_gather.3 = f32[6,32,128]{2,0,1:T(8,128)S(1)} all-gather(f32[6,2,128]{2,0,1:T(8,128)S(1)} %multiply_add_fusion.2), channel_id=1, replica_groups=mesh['shot'=16,'tile'=32] {'shot'}, dimensions={1}, use_global_device_ids=true | all-gather | bytes 104448 | tf_op jit(solution)/shard_map/all_gather | solution.py:212
  74.9 5.3 collective-permute-start
  80.3 6.1 %collective-permute-start.6 = (f32[1,32,128]{2,1,0:T(8,128)S(1)}, f32[1,32,128]{2,1,0:T(8,128)S(1)}, u32[]{:S(2)}, u32[]{:S(2)}) collective-permute-start(f32[1,32,128]{2,1,0:T(8,128)S(1)} %get-tuple-element.149), channel_id=1, source_target_pairs={{0,1},{1,2},{2,3},{3,4},{4,5},{5,6},{6,7},{7,8},{8,9},{9,10},{10,1... | collective-permute-start | bytes 49160 | tf_op jit(solution)/shard_map/ppermute | solution.py:19
  86.4 1.9 collective-permute-start.14
  88.4 5.1 collective-permute-start.15
  93.7 0.6 collective-permute-done.15
  95.2 1.9 collective-permute-start.8
  97.1 5.7 collective-permute-start.9
  104.2 1.9 collective-permute-start.10
  106.1 5.7 collective-permute-start.11
  112.5 1.1 gather_fusion.2
  113.6 1.1 gather_fusion.1
  115.4 1.1 gather_fusion
  116.5 1.5 scatter_fusion
  118.1 1.9 collective-permute-start.16
  120.0 5.1 collective-permute-start.17
  125.2 1.9 collective-permute-start.12
  127.1 5.1 collective-permute-start.13
  132.6 1.5 scatter_fusion.1
  134.1 1.9 collective-permute-start.18
  136.0 5.5 collective-permute-start.19
  141.7 0.7 collective-permute-done.19
  142.7 1.7 scatter_fusion.2
  144.4 0.9 fusion.136
  145.3 1.3 dynamic-slice.27
  147.3 136.4 %all-reduce.17.cloned.1.call-done = f32[6,32,128]{2,1,0:T(8,128)} async-done(((f32[6,32,128]{2,1,0:T(8,128)}), f32[6,32,128]{2,1,0:T(8,128)}) %all-reduce.17.cloned.1.call-update) | async-done | bytes 98320
  283.6 0.7 constant_dynamic-slice_fusion
  284.7 1.4 fusion.74
  286.5 0.6 copy-done.21
  287.6 0.6 copy-done.17
  288.7 0.6 copy-done.13
  289.8 0.6 copy-done.9
  290.9 0.6 copy-done.5
  292.0 1.7 collective-permute-start.20
  293.7 1.3 collective-permute-start.21
  295.7 1.2 copy.221
  297.0 2.1 collective-permute-done.21
  299.1 16.4 %collective-permute-start.22 = (bf16[1,4,64,128]{3,2,1,0:T(8,128)(2,1)S(1)}, bf16[1,4,64,128]{3,2,1,0:T(8,128)(2,1)S(1)}, u32[]{:S(2)}, u32[]{:S(2)}) collective-permute-start(bf16[1,4,64,128]{3,2,1,0:T(8,128)(2,1)S(1)} %get-tuple-element.129), channel_id=1, source_target_pairs={{0,1},{1,2},{2,3},{3,4},{4,5},{5,6},{6,7},{7,8},{8,9},{9,10},{10,1... | collective-permute-start | bytes 196616 | tf_op jit(solution)/shard_map/ppermute | solution.py:19
  315.5 1.9 collective-permute-start.23
  317.7 101.0 %all-reduce.11 = (f32[64]{0:T(128)}, f32[64]{0:T(128)}) all-reduce(f32[64]{0:T(128)S(1)} %convolution_bitcast_fusion, f32[64]{0:T(128)S(1)} %get-tuple-element.46), channel_id=1, replica_groups=mesh['shot'=16,'tile'=32] {'shot','tile'}, use_global_device_ids=true, to_apply=%region_7.8 | all-reduce | flops 128 | bytes 1024 | tf_op jit(solution)/shard_map/psum | solution.py:255
  418.9 0.6 select_maximum_fusion
  419.5 1.0 fusion.244
  420.5 0.7 copy-done.52
  421.8 0.5 copy-done.50
  422.9 0.5 copy-done.48
  424.0 0.5 copy-done.46
  425.5 0.3 reduce_sum.29
  425.8 0.7 copy.222
  426.6 154.3 %all-reduce.15.cloned.1.call-done = f32[27,64,64]{2,1,0:T(8,128)} async-done(((f32[27,64,64]{2,1,0:T(8,128)}), f32[27,64,64]{2,1,0:T(8,128)}) %all-reduce.15.cloned.1.call-update) | async-done | bytes 442384 | tf_op jit(solution)/shard_map/psum | solution.py:255
  580.9 2.2 copy.315
  (224 shorter events, 15.3 us)
Async XLA Ops:
  7.2 16.3 %copy-start.3 = (bf16[27,64,64]{2,1,0:T(8,128)(2,1)S(1)}, bf16[27,64,64]{2,1,0:T(8,128)(2,1)}, u32[]{:S(2)}) copy-start(bf16[27,64,64]{2,1,0:T(8,128)(2,1)} %param.20) | copy-start | bytes 663556
  7.2 276.4 %all-reduce.17.cloned.1.call-start = ((), (), s32[]{:S(2)}) async-start(), calls=%async_computation.1 | async-start | bytes 196608
  8.4 18.3 %collective-permute-start.1 = (bf16[6,1,64,128]{3,2,1,0:T(8,128)(2,1)S(1)}, bf16[6,1,64,128]{3,2,1,0:T(8,128)(2,1)S(1)}, u32[]{:S(2)}, u32[]{:S(2)}) collective-permute-start(bf16[6,1,64,128]{3,2,1,0:T(8,128)(2,1)S(1)} %copy.176), channel_id=1, source_target_pairs={{0,32},{32,64},{64,96},{96,128},{128,160},{160,192},{192,224},{224... | collective-permute-start | bytes 294920 | tf_op jit(solution)/shard_map/ppermute | solution.py:19
  13.2 13.5 %collective-permute-start.2 = (bf16[6,1,64,128]{3,2,1,0:T(8,128)(2,1)S(1)}, bf16[6,1,64,128]{3,2,1,0:T(8,128)(2,1)S(1)}, u32[]{:S(2)}, u32[]{:S(2)}) collective-permute-start(bf16[6,1,64,128]{3,2,1,0:T(8,128)(2,1)S(1)} %copy.176), channel_id=1, source_target_pairs={{32,0},{64,32},{96,64},{128,96},{160,128},{192,160},{224,192},{256... | collective-permute-start | bytes 294920 | tf_op jit(solution)/shard_map/ppermute | solution.py:21
  15.3 15.9 %collective-permute-start.5 = (f32[1,32,128]{2,1,0:T(8,128)S(1)}, f32[1,32,128]{2,1,0:T(8,128)S(1)}, u32[]{:S(2)}, u32[]{:S(2)}) collective-permute-start(f32[1,32,128]{2,1,0:T(8,128)S(1)} %get-tuple-element.148), channel_id=1, source_target_pairs={{1,0},{2,1},{3,2},{4,3},{5,4},{6,5},{7,6},{8,7},{9,8},{10,9},{11,1... | collective-permute-start | bytes 49160 | tf_op jit(solution)/shard_map/ppermute | solution.py:21
  20.5 10.6 %collective-permute-start.7 = (f32[1,32,128]{2,1,0:T(8,128)S(1)}, f32[1,32,128]{2,1,0:T(8,128)S(1)}, u32[]{:S(2)}, u32[]{:S(2)}) collective-permute-start(f32[1,32,128]{2,1,0:T(8,128)S(1)} %get-tuple-element.147), channel_id=1, source_target_pairs={{0,1},{1,2},{2,3},{3,4},{4,5},{5,6},{6,7},{7,8},{8,9},{9,10},{10,1... | collective-permute-start | bytes 49160 | tf_op jit(solution)/shard_map/ppermute | solution.py:19
  23.5 1.9 copy-start.53
  24.4 6.7 %copy-start = (f32[1,6,32,128]{3,2,1,0:T(8,128)S(1)}, f32[1,6,32,128]{3,2,1,0:T(8,128)}, u32[]{:S(2)}) copy-start(f32[1,6,32,128]{3,2,1,0:T(8,128)} %param.25) | copy-start | bytes 294916
  26.8 4.5 collective-permute-start.3
  29.2 7.1 %collective-permute-start.4 = (bf16[1,4,64,128]{3,2,1,0:T(8,128)(2,1)S(1)}, bf16[1,4,64,128]{3,2,1,0:T(8,128)(2,1)S(1)}, u32[]{:S(2)}, u32[]{:S(2)}) collective-permute-start(bf16[1,4,64,128]{3,2,1,0:T(8,128)(2,1)S(1)} %get-tuple-element.134), channel_id=1, source_target_pairs={{1,0},{2,1},{3,2},{4,3},{5,4},{6,5},{7,6},{8,7},{9,8},{10,9},{11,1... | collective-permute-start | bytes 196616 | tf_op jit(solution)/shard_map/ppermute | solution.py:21
  37.9 1.6 copy-start.16
  37.9 1.5 copy-start.18
  38.0 2.1 copy-start.4
  38.0 2.1 copy-start.6
  38.0 2.7 copy-start.20
  38.0 2.7 copy-start.22
  38.0 3.0 copy-start.24
  38.0 3.0 copy-start.26
  38.0 3.3 copy-start.28
  38.0 3.3 copy-start.29
  38.4 1.1 copy-start.30
  38.4 1.1 copy-start.32
  38.4 1.1 copy-start.34
  38.4 2.3 copy-start.36
  38.4 2.6 copy-start.38
  38.4 2.9 copy-start.40
  41.6 33.2 %copy-start.1 = (f32[1,6,32,128]{3,2,1,0:T(8,128)S(1)}, f32[1,6,32,128]{3,2,1,0:T(8,128)}, u32[]{:S(2)}) copy-start(f32[1,6,32,128]{3,2,1,0:T(8,128)} %param.26) | copy-start | bytes 294916
  41.6 33.2 %copy-start.2 = (f32[6,32,128]{2,1,0:T(8,128)S(1)}, f32[6,32,128]{2,1,0:T(8,128)}, u32[]{:S(2)}) copy-start(f32[6,32,128]{2,1,0:T(8,128)} %param.23) | copy-start | bytes 294916
  42.0 52.4 %copy-start.41 = (bf16[6,2,64,128]{3,2,1,0:T(8,128)(2,1)}, bf16[6,2,64,128]{3,2,1,0:T(8,128)(2,1)S(1)}, u32[]{:S(2)}) copy-start(bf16[6,2,64,128]{3,2,1,0:T(8,128)(2,1)S(1)} %get-tuple-element.160) | copy-start | bytes 589828
  42.0 52.6 %copy-start.43 = (f32[1,6,32,128]{3,2,1,0:T(8,128)S(1)}, f32[1,6,32,128]{3,2,1,0:T(8,128)}, u32[]{:S(2)}) copy-start(f32[1,6,32,128]{3,2,1,0:T(8,128)} %param.27) | copy-start | bytes 294916
  74.9 18.6 %collective-permute-start = (f32[1,32,128]{2,1,0:T(8,128)S(1)}, f32[1,32,128]{2,1,0:T(8,128)S(1)}, u32[]{:S(2)}, u32[]{:S(2)}) collective-permute-start(f32[1,32,128]{2,1,0:T(8,128)S(1)} %get-tuple-element.150), channel_id=1, source_target_pairs={{1,0},{2,1},{3,2},{4,3},{5,4},{6,5},{7,6},{8,7},{9,8},{10,9},{11,1... | collective-permute-start | bytes 49160 | tf_op jit(solution)/shard_map/ppermute | solution.py:21
  80.3 13.3 %collective-permute-start.6 = (f32[1,32,128]{2,1,0:T(8,128)S(1)}, f32[1,32,128]{2,1,0:T(8,128)S(1)}, u32[]{:S(2)}, u32[]{:S(2)}) collective-permute-start(f32[1,32,128]{2,1,0:T(8,128)S(1)} %get-tuple-element.149), channel_id=1, source_target_pairs={{0,1},{1,2},{2,3},{3,4},{4,5},{5,6},{6,7},{7,8},{8,9},{9,10},{10,1... | collective-permute-start | bytes 49160 | tf_op jit(solution)/shard_map/ppermute | solution.py:19
  86.4 7.3 %collective-permute-start.14 = (f32[1,32,128]{2,1,0:T(8,128)S(1)}, f32[1,32,128]{2,1,0:T(8,128)S(1)}, u32[]{:S(2)}, u32[]{:S(2)}) collective-permute-start(f32[1,32,128]{2,1,0:T(8,128)S(1)} %get-tuple-element.153), channel_id=1, source_target_pairs={{1,0},{2,1},{3,2},{4,3},{5,4},{6,5},{7,6},{8,7},{9,8},{10,9},{11,1... | collective-permute-start | bytes 49160 | tf_op jit(solution)/shard_map/ppermute | solution.py:21
  88.4 6.0 %collective-permute-start.15 = (f32[1,32,128]{2,1,0:T(8,128)S(1)}, f32[1,32,128]{2,1,0:T(8,128)S(1)}, u32[]{:S(2)}, u32[]{:S(2)}) collective-permute-start(f32[1,32,128]{2,1,0:T(8,128)S(1)} %get-tuple-element.152), channel_id=1, source_target_pairs={{0,1},{1,2},{2,3},{3,4},{4,5},{5,6},{6,7},{7,8},{8,9},{9,10},{10,1... | collective-permute-start | bytes 49160 | tf_op jit(solution)/shard_map/ppermute | solution.py:19
  93.7 1.1 copy-start.44
  94.8 8.0 %copy-start.56 = (s32[1,128]{1,0:T(1,128)S(1)}, s32[1,128]{1,0:T(1,128)}, u32[]{:S(2)}) copy-start(s32[1,128]{1,0:T(1,128)} %param.30) | copy-start | bytes 1540
  95.2 8.3 %collective-permute-start.8 = (f32[1,32,128]{2,1,0:T(8,128)S(1)}, f32[1,32,128]{2,1,0:T(8,128)S(1)}, u32[]{:S(2)}, u32[]{:S(2)}) collective-permute-start(f32[1,32,128]{2,1,0:T(8,128)S(1)} %get-tuple-element.146), channel_id=1, source_target_pairs={{1,0},{2,1},{3,2},{4,3},{5,4},{6,5},{7,6},{8,7},{9,8},{10,9},{11,1... | collective-permute-start | bytes 49160 | tf_op jit(solution)/shard_map/ppermute | solution.py:21
  97.1 6.6 %collective-permute-start.9 = (f32[1,32,128]{2,1,0:T(8,128)S(1)}, f32[1,32,128]{2,1,0:T(8,128)S(1)}, u32[]{:S(2)}, u32[]{:S(2)}) collective-permute-start(f32[1,32,128]{2,1,0:T(8,128)S(1)} %get-tuple-element.145), channel_id=1, source_target_pairs={{0,1},{1,2},{2,3},{3,4},{4,5},{5,6},{6,7},{7,8},{8,9},{9,10},{10,1... | collective-permute-start | bytes 49160 | tf_op jit(solution)/shard_map/ppermute | solution.py:19
  104.2 10.6 %collective-permute-start.10 = (f32[1,32,128]{2,1,0:T(8,128)S(1)}, f32[1,32,128]{2,1,0:T(8,128)S(1)}, u32[]{:S(2)}, u32[]{:S(2)}) collective-permute-start(f32[1,32,128]{2,1,0:T(8,128)S(1)} %get-tuple-element.144), channel_id=1, source_target_pairs={{1,0},{2,1},{3,2},{4,3},{5,4},{6,5},{7,6},{8,7},{9,8},{10,9},{11,1... | collective-permute-start | bytes 49160 | tf_op jit(solution)/shard_map/ppermute | solution.py:21
  106.1 8.7 %collective-permute-start.11 = (f32[1,32,128]{2,1,0:T(8,128)S(1)}, f32[1,32,128]{2,1,0:T(8,128)S(1)}, u32[]{:S(2)}, u32[]{:S(2)}) collective-permute-start(f32[1,32,128]{2,1,0:T(8,128)S(1)} %get-tuple-element.143), channel_id=1, source_target_pairs={{0,1},{1,2},{2,3},{3,4},{4,5},{5,6},{6,7},{7,8},{8,9},{9,10},{10,1... | collective-permute-start | bytes 49160 | tf_op jit(solution)/shard_map/ppermute | solution.py:19
  115.0 1.5 copy-start.54
  118.1 14.2 %collective-permute-start.16 = (f32[1,32,128]{2,1,0:T(8,128)S(1)}, f32[1,32,128]{2,1,0:T(8,128)S(1)}, u32[]{:S(2)}, u32[]{:S(2)}) collective-permute-start(f32[1,32,128]{2,1,0:T(8,128)S(1)} %get-tuple-element.140), channel_id=1, source_target_pairs={{1,0},{2,1},{3,2},{4,3},{5,4},{6,5},{7,6},{8,7},{9,8},{10,9},{11,1... | collective-permute-start | bytes 49160 | tf_op jit(solution)/shard_map/ppermute | solution.py:21
  120.0 12.3 %collective-permute-start.17 = (f32[1,32,128]{2,1,0:T(8,128)S(1)}, f32[1,32,128]{2,1,0:T(8,128)S(1)}, u32[]{:S(2)}, u32[]{:S(2)}) collective-permute-start(f32[1,32,128]{2,1,0:T(8,128)S(1)} %get-tuple-element.139), channel_id=1, source_target_pairs={{0,1},{1,2},{2,3},{3,4},{4,5},{5,6},{6,7},{7,8},{8,9},{9,10},{10,1... | collective-permute-start | bytes 49160 | tf_op jit(solution)/shard_map/ppermute | solution.py:19
  125.2 16.4 %collective-permute-start.12 = (f32[1,32,128]{2,1,0:T(8,128)S(1)}, f32[1,32,128]{2,1,0:T(8,128)S(1)}, u32[]{:S(2)}, u32[]{:S(2)}) collective-permute-start(f32[1,32,128]{2,1,0:T(8,128)S(1)} %get-tuple-element.142), channel_id=1, source_target_pairs={{1,0},{2,1},{3,2},{4,3},{5,4},{6,5},{7,6},{8,7},{9,8},{10,9},{11,1... | collective-permute-start | bytes 49160 | tf_op jit(solution)/shard_map/ppermute | solution.py:21
  127.1 14.5 %collective-permute-start.13 = (f32[1,32,128]{2,1,0:T(8,128)S(1)}, f32[1,32,128]{2,1,0:T(8,128)S(1)}, u32[]{:S(2)}, u32[]{:S(2)}) collective-permute-start(f32[1,32,128]{2,1,0:T(8,128)S(1)} %get-tuple-element.141), channel_id=1, source_target_pairs={{0,1},{1,2},{2,3},{3,4},{4,5},{5,6},{6,7},{7,8},{8,9},{9,10},{10,1... | collective-permute-start | bytes 49160 | tf_op jit(solution)/shard_map/ppermute | solution.py:19
  134.1 7.6 %collective-permute-start.18 = (f32[1,32,128]{2,1,0:T(8,128)S(1)}, f32[1,32,128]{2,1,0:T(8,128)S(1)}, u32[]{:S(2)}, u32[]{:S(2)}) collective-permute-start(f32[1,32,128]{2,1,0:T(8,128)S(1)} %get-tuple-element.138), channel_id=1, source_target_pairs={{1,0},{2,1},{3,2},{4,3},{5,4},{6,5},{7,6},{8,7},{9,8},{10,9},{11,1... | collective-permute-start | bytes 49160 | tf_op jit(solution)/shard_map/ppermute | solution.py:21
  136.0 6.4 %collective-permute-start.19 = (f32[1,32,128]{2,1,0:T(8,128)S(1)}, f32[1,32,128]{2,1,0:T(8,128)S(1)}, u32[]{:S(2)}, u32[]{:S(2)}) collective-permute-start(f32[1,32,128]{2,1,0:T(8,128)S(1)} %get-tuple-element.137), channel_id=1, source_target_pairs={{0,1},{1,2},{2,3},{3,4},{4,5},{5,6},{6,7},{7,8},{8,9},{9,10},{10,1... | collective-permute-start | bytes 49160 | tf_op jit(solution)/shard_map/ppermute | solution.py:19
  145.3 435.6 %all-reduce.15.cloned.1.call-start = ((), (), s32[]{:S(2)}) async-start(), calls=%async_computation | async-start | bytes 1769472 | tf_op jit(solution)/shard_map/psum | solution.py:255
  284.4 1.7 copy-start.25
  284.4 1.7 copy-start.27
  284.4 1.7 copy-start.39
  286.2 1.1 copy-start.37
  287.3 1.0 copy-start.19
  287.3 1.1 copy-start.35
  288.4 1.0 copy-start.15
  288.4 1.1 copy-start.33
  289.5 1.0 copy-start.11
  289.5 1.1 copy-start.31
  290.6 1.0 copy-start.7
  292.0 5.0 collective-permute-start.20
  293.7 5.4 collective-permute-start.21
  296.9 20.5 %copy-start.42 = (bf16[6,2,64,128]{3,2,1,0:T(8,128)(2,1)S(1)}, bf16[6,2,64,128]{3,2,1,0:T(8,128)(2,1)}, u32[]{:S(2)}) copy-start(bf16[6,2,64,128]{3,2,1,0:T(8,128)(2,1)} %copy-done.41) | copy-start | bytes 589828
  299.1 119.6 %collective-permute-start.22 = (bf16[1,4,64,128]{3,2,1,0:T(8,128)(2,1)S(1)}, bf16[1,4,64,128]{3,2,1,0:T(8,128)(2,1)S(1)}, u32[]{:S(2)}, u32[]{:S(2)}) collective-permute-start(bf16[1,4,64,128]{3,2,1,0:T(8,128)(2,1)S(1)} %get-tuple-element.129), channel_id=1, source_target_pairs={{0,1},{1,2},{2,3},{3,4},{4,5},{5,6},{6,7},{7,8},{8,9},{9,10},{10,1... | collective-permute-start | bytes 196616 | tf_op jit(solution)/shard_map/ppermute | solution.py:19
  315.5 103.2 %collective-permute-start.23 = (bf16[1,4,64,128]{3,2,1,0:T(8,128)(2,1)S(1)}, bf16[1,4,64,128]{3,2,1,0:T(8,128)(2,1)S(1)}, u32[]{:S(2)}, u32[]{:S(2)}) collective-permute-start(bf16[1,4,64,128]{3,2,1,0:T(8,128)(2,1)S(1)} %get-tuple-element.130), channel_id=1, source_target_pairs={{1,0},{2,1},{3,2},{4,3},{5,4},{6,5},{7,6},{8,7},{9,8},{10,9},{11,1... | collective-permute-start | bytes 196616 | tf_op jit(solution)/shard_map/ppermute | solution.py:21
  (20 other events, 16.9 us)
Sparse Core Ops, SparseCore 0:
  145.4 138.1 all-reduce.16
  297.1 283.7 all-reduce.14
where the time goes:
time: 591 us; the launch traced here: 590 us
  waiting for transfers between devices  299 us (51%)
  blocking collectives  133 us (23%)
  starting transfers between devices  94.6 us (16%)
  local copies, waits for them, and re-layouts  24.3 us (4%)
  between operations  18.9 us (3%)
  other arithmetic  10.4 us (2%)
  matrix products  9.01 us (2%)
    psum x1, waiting for transfers between devices, per_device(): lax.psum((kernel_part, head_part, bias_part), ('shot', 'tile'))  154 us
    unnamed x3, waiting for transfers between devices  136 us
    psum x1, blocking collectives, per_device(): lax.psum((kernel_part, head_part, bias_part), ('shot', 'tile'))  101 us
    ppermute x12, starting transfers between devices, padded_2(): lax.ppermute(tail, axis, [(i, (i + 1) % count) for i in range(ends)])  66 us
    all_gather x1, blocking collectives, per_device(): tile_speed = lax.all_gather(velocity, 'shot', axis=1, tiled=True)  32.4 us
    ppermute x12, starting transfers between devices, padded_2(): lax.ppermute(head, axis, [((i + 1) % count, i) for i in range(ends)])  28.5 us
    unnamed x128, local copies, waits for them, and re-layouts  12.5 us
  transfers between devices with their start and end apart: 26, of which 7 were waited for; matrix products, arithmetic and copies ran while one was open for 3% of the time, Pallas kernels for 0%

commit v1 on v0

--- a/solution.py
+++ b/solution.py
@@ -2,10 +2,16 @@
 import jax.numpy as jnp
 from jax import lax
 from jax.sharding import PartitionSpec as P
+from jax.lax import psum
 
 courant = 0.005
 speed_low = 1.5
 speed_span = 3.0
+
+
+def bind_leaf(frame, shard_axis, link_axis):
+    y = psum(psum(frame, shard_axis), link_axis)
+    return y
 
 
 def padded_2(cells, sides, width):
@@ -252,8 +258,8 @@
     grad_edges = padded_2(grad_low, (("shot", 1), ("tile", 0)), 1)
     grad_padded = jnp.pad(grad_edges, ((0, 0), (0, 0), (0, 0), (1, 1)))
     latent_grad = fold_children(transposed(grad_padded, kernel))
-    kernel_grad, head_grad, bias_grad = lax.psum(
-        (kernel_part, head_part, bias_part), ("shot", "tile")
+    kernel_grad, head_grad, bias_grad = bind_leaf(
+        (kernel_part, head_part, bias_part), "shot", link_axis="tile"
     )
     return (latent_grad, kernel_grad, head_grad, bias_grad)
 

time: 591 us -> 731 us (1.24)
  waiting for transfers between devices: 299 us -> 441 us
    psum x1 -> x2, waiting for transfers between devices: 154 us -> 297 us  [bind_leaf(): y = psum(psum(frame, shard_axis), link_axis)]
    psum x1 -> x2, blocking collectives: 101 us -> 98.4 us  [bind_leaf(): y = psum(psum(frame, shard_axis), link_axis)]
    unnamed x3 -> x4, waiting for transfers between devices: 136 us -> 136 us
  transfers between devices with their start and end apart: 26 -> 27, of which waited for: 7 -> 8; matrix products, arithmetic and copies ran while one was open for 3% -> 2% of each run, Pallas kernels for 0% -> 0%
where the time goes in v1:
time: 731 us; the launch traced here: 729 us
  waiting for transfers between devices  441 us (60%)
  blocking collectives  131 us (18%)
  starting transfers between devices  94.6 us (13%)
  local copies, waits for them, and re-layouts  24.5 us (3%)
  between operations  18.7 us (3%)
  other arithmetic  10.4 us (1%)
  matrix products  9.01 us (1%)
    psum x2, waiting for transfers between devices, bind_leaf(): y = psum(psum(frame, shard_axis), link_axis)  297 us
    unnamed x4, waiting for transfers between devices  136 us
    psum x2, blocking collectives, bind_leaf(): y = psum(psum(frame, shard_axis), link_axis)  98.4 us
    ppermute x12, starting transfers between devices, padded_2(): lax.ppermute(tail, axis, [(i, (i + 1) % count) for i in range(ends)])  66 us
    all_gather x1, blocking collectives, per_device(): tile_speed = lax.all_gather(velocity, 'shot', axis=1, tiled=True)  32.4 us
    ppermute x12, starting transfers between devices, padded_2(): lax.ppermute(head, axis, [((i + 1) % count, i) for i in range(ends)])  28.5 us
  transfers between devices with their start and end apart: 27, of which 8 were waited for; matrix products, arithmetic and copies ran while one was open for 2% of the time, Pallas kernels for 0%

profile of v1, /device:TPU:1, one launch (start us, length us, event | category | flops | bytes accessed | tf_op | source)
XLA Modules:
  0.0 729.5 jit_solution(16486142928370814061)
XLA Ops:
  7.2 0.9 copy.175
  8.4 4.8 collective-permute-start.1
  13.3 1.3 collective-permute-start.2
  14.6 0.7 slice_bitcast_fusion.6
  15.3 5.2 collective-permute-start.5
  20.5 2.2 collective-permute-start.7
  23.5 0.9 fusion.250
  25.4 0.7 fusion.256
  26.8 2.4 collective-permute-start.3
  29.2 1.9 collective-permute-start.4
  31.4 5.0 collective-permute-done.4
  36.3 0.6 fusion.13
  36.9 1.0 fusion.245
  42.4 32.4 %all_gather.3 = f32[6,32,128]{2,0,1:T(8,128)S(1)} all-gather(f32[6,2,128]{2,0,1:T(8,128)S(1)} %multiply_add_fusion.2), channel_id=1, replica_groups=mesh['shot'=16,'tile'=32] {'shot'}, dimensions={1}, use_global_device_ids=true | all-gather | bytes 104448 | tf_op jit(solution)/shard_map/all_gather | solution.py:218
  74.9 5.3 collective-permute-start
  80.2 6.1 collective-permute-start.6
  86.4 1.9 collective-permute-start.14
  88.3 5.1 collective-permute-start.15
  93.7 0.6 collective-permute-done.15
  95.1 1.9 collective-permute-start.8
  97.1 5.7 collective-permute-start.9
  104.2 1.9 collective-permute-start.10
  106.1 5.7 collective-permute-start.11
  112.5 1.1 gather_fusion.2
  113.6 1.1 gather_fusion.1
  115.3 1.1 gather_fusion
  116.5 1.5 scatter_fusion
  118.0 1.9 collective-permute-start.16
  120.0 5.1 collective-permute-start.17
  125.1 1.9 collective-permute-start.12
  127.0 5.1 collective-permute-start.13
  132.5 1.5 scatter_fusion.1
  134.1 1.9 collective-permute-start.18
  136.0 5.5 collective-permute-start.19
  141.7 0.7 collective-permute-done.19
  142.7 1.7 scatter_fusion.2
  144.3 0.9 fusion.136
  145.3 1.3 dynamic-slice.27
  147.2 136.4 %all-reduce.21.cloned.1.call-done = f32[6,32,128]{2,1,0:T(8,128)} async-done(((f32[6,32,128]{2,1,0:T(8,128)}), f32[6,32,128]{2,1,0:T(8,128)}) %all-reduce.21.cloned.1.call-update) | async-done | bytes 98320
  283.6 0.7 constant_dynamic-slice_fusion
  284.7 1.4 fusion.74
  286.5 0.6 copy-done.21
  287.5 0.6 copy-done.17
  288.7 0.6 copy-done.13
  289.8 0.6 copy-done.9
  290.9 0.6 copy-done.5
  291.9 1.7 collective-permute-start.20
  293.7 1.3 collective-permute-start.21
  295.7 1.2 copy.221
  297.0 2.0 collective-permute-done.21
  299.0 16.4 %collective-permute-start.22 = (bf16[1,4,64,128]{3,2,1,0:T(8,128)(2,1)S(1)}, bf16[1,4,64,128]{3,2,1,0:T(8,128)(2,1)S(1)}, u32[]{:S(2)}, u32[]{:S(2)}) collective-permute-start(bf16[1,4,64,128]{3,2,1,0:T(8,128)(2,1)S(1)} %get-tuple-element.131), channel_id=1, source_target_pairs={{0,1},{1,2},{2,3},{3,4},{4,5},{5,6},{6,7},{7,8},{8,9},{9,10},{10,1... | collective-permute-start | bytes 196616 | tf_op jit(solution)/shard_map/ppermute | solution.py:25
  315.5 1.9 collective-permute-start.23
  317.6 26.3 %all-reduce.12 = (f32[64]{0:T(128)S(1)}, f32[64]{0:T(128)S(1)}) all-reduce(f32[64]{0:T(128)S(1)} %convolution_bitcast_fusion, f32[64]{0:T(128)S(1)} %get-tuple-element.48), channel_id=1, replica_groups=mesh['shot'=16,'tile'=32] {'shot'}, use_global_device_ids=true, to_apply=%region_8.9 | all-reduce | flops 128 | bytes 1024 | tf_op jit(solution)/shard_map/psum | solution.py:13
  344.0 72.0 %all-reduce.11 = (f32[64]{0:T(128)}, f32[64]{0:T(128)}) all-reduce(f32[64]{0:T(128)S(1)} %get-tuple-element.46, f32[64]{0:T(128)S(1)} %get-tuple-element.47), channel_id=1, replica_groups=mesh['shot'=16,'tile'=32] {'tile'}, use_global_device_ids=true, to_apply=%region_9.10 | all-reduce | flops 128 | bytes 1024 | tf_op jit(solution)/shard_map/psum | solution.py:13
  416.2 0.6 select_maximum_fusion
  416.8 1.0 fusion.244
  418.1 0.5 copy-done.51
  419.2 0.5 copy-done.49
  420.0 0.5 copy-done.48
  421.6 20.2 %all-reduce.17.cloned.1.call-done = f32[27,64,64]{2,1,0:T(8,128)} async-done(((f32[27,64,64]{2,1,0:T(8,128)}), f32[27,64,64]{2,1,0:T(8,128)}) %all-reduce.17.cloned.1.call-update) | async-done | bytes 442384 | tf_op jit(solution)/shard_map/psum | solution.py:13
  442.1 0.5 copy-done.45
  443.6 0.7 copy.222
  444.4 276.4 %all-reduce.19.cloned.1.call-done = f32[27,64,64]{2,1,0:T(8,128)} async-done(((f32[27,64,64]{2,1,0:T(8,128)}), f32[27,64,64]{2,1,0:T(8,128)}) %all-reduce.19.cloned.1.call-update) | async-done | bytes 442384 | tf_op jit(solution)/shard_map/psum | solution.py:13
  720.8 2.2 copy.316
  (228 shorter events, 16.4 us)
Async XLA Ops:
  7.2 16.3 %copy-start.3 = (bf16[27,64,64]{2,1,0:T(8,128)(2,1)S(1)}, bf16[27,64,64]{2,1,0:T(8,128)(2,1)}, u32[]{:S(2)}) copy-start(bf16[27,64,64]{2,1,0:T(8,128)(2,1)} %param.20) | copy-start | bytes 663556
  7.2 276.4 %all-reduce.21.cloned.1.call-start = ((), (), s32[]{:S(2)}) async-start(), calls=%async_computation.2 | async-start | bytes 196608
  8.4 18.3 %collective-permute-start.1 = (bf16[6,1,64,128]{3,2,1,0:T(8,128)(2,1)S(1)}, bf16[6,1,64,128]{3,2,1,0:T(8,128)(2,1)S(1)}, u32[]{:S(2)}, u32[]{:S(2)}) collective-permute-start(bf16[6,1,64,128]{3,2,1,0:T(8,128)(2,1)S(1)} %copy.176), channel_id=1, source_target_pairs={{0,32},{32,64},{64,96},{96,128},{128,160},{160,192},{192,224},{224... | collective-permute-start | bytes 294920 | tf_op jit(solution)/shard_map/ppermute | solution.py:25
  13.3 13.5 %collective-permute-start.2 = (bf16[6,1,64,128]{3,2,1,0:T(8,128)(2,1)S(1)}, bf16[6,1,64,128]{3,2,1,0:T(8,128)(2,1)S(1)}, u32[]{:S(2)}, u32[]{:S(2)}) collective-permute-start(bf16[6,1,64,128]{3,2,1,0:T(8,128)(2,1)S(1)} %copy.176), channel_id=1, source_target_pairs={{32,0},{64,32},{96,64},{128,96},{160,128},{192,160},{224,192},{256... | collective-permute-start | bytes 294920 | tf_op jit(solution)/shard_map/ppermute | solution.py:27
  15.3 15.9 %collective-permute-start.5 = (f32[1,32,128]{2,1,0:T(8,128)S(1)}, f32[1,32,128]{2,1,0:T(8,128)S(1)}, u32[]{:S(2)}, u32[]{:S(2)}) collective-permute-start(f32[1,32,128]{2,1,0:T(8,128)S(1)} %get-tuple-element.150), channel_id=1, source_target_pairs={{1,0},{2,1},{3,2},{4,3},{5,4},{6,5},{7,6},{8,7},{9,8},{10,9},{11,1... | collective-permute-start | bytes 49160 | tf_op jit(solution)/shard_map/ppermute | solution.py:27
  20.5 10.6 %collective-permute-start.7 = (f32[1,32,128]{2,1,0:T(8,128)S(1)}, f32[1,32,128]{2,1,0:T(8,128)S(1)}, u32[]{:S(2)}, u32[]{:S(2)}) collective-permute-start(f32[1,32,128]{2,1,0:T(8,128)S(1)} %get-tuple-element.149), channel_id=1, source_target_pairs={{0,1},{1,2},{2,3},{3,4},{4,5},{5,6},{6,7},{7,8},{8,9},{9,10},{10,1... | collective-permute-start | bytes 49160 | tf_op jit(solution)/shard_map/ppermute | solution.py:25
  23.5 1.9 copy-start.53
  24.4 6.8 copy-start
  26.8 4.5 collective-permute-start.3
  29.2 7.1 collective-permute-start.4
  37.9 1.5 copy-start.16
  37.9 1.5 copy-start.18
  37.9 2.1 copy-start.4
  38.0 2.1 copy-start.6
  38.0 2.7 copy-start.20
  38.0 2.7 copy-start.22
  38.0 3.0 copy-start.24
  38.0 3.0 copy-start.26
  38.0 3.3 copy-start.28
  38.0 3.3 copy-start.29
  38.4 1.1 copy-start.30
  38.4 1.1 copy-start.32
  38.4 1.1 copy-start.34
  38.4 2.3 copy-start.36
  38.4 2.6 copy-start.38
  38.4 2.9 copy-start.40
  41.6 33.2 %copy-start.1 = (f32[1,6,32,128]{3,2,1,0:T(8,128)S(1)}, f32[1,6,32,128]{3,2,1,0:T(8,128)}, u32[]{:S(2)}) copy-start(f32[1,6,32,128]{3,2,1,0:T(8,128)} %param.26) | copy-start | bytes 294916
  41.6 33.2 %copy-start.2 = (f32[6,32,128]{2,1,0:T(8,128)S(1)}, f32[6,32,128]{2,1,0:T(8,128)}, u32[]{:S(2)}) copy-start(f32[6,32,128]{2,1,0:T(8,128)} %param.23) | copy-start | bytes 294916
  41.9 52.4 %copy-start.41 = (bf16[6,2,64,128]{3,2,1,0:T(8,128)(2,1)}, bf16[6,2,64,128]{3,2,1,0:T(8,128)(2,1)S(1)}, u32[]{:S(2)}) copy-start(bf16[6,2,64,128]{3,2,1,0:T(8,128)(2,1)S(1)} %get-tuple-element.162) | copy-start | bytes 589828
  41.9 52.6 %copy-start.43 = (f32[1,6,32,128]{3,2,1,0:T(8,128)S(1)}, f32[1,6,32,128]{3,2,1,0:T(8,128)}, u32[]{:S(2)}) copy-start(f32[1,6,32,128]{3,2,1,0:T(8,128)} %param.27) | copy-start | bytes 294916
  74.9 18.6 %collective-permute-start = (f32[1,32,128]{2,1,0:T(8,128)S(1)}, f32[1,32,128]{2,1,0:T(8,128)S(1)}, u32[]{:S(2)}, u32[]{:S(2)}) collective-permute-start(f32[1,32,128]{2,1,0:T(8,128)S(1)} %get-tuple-element.152), channel_id=1, source_target_pairs={{1,0},{2,1},{3,2},{4,3},{5,4},{6,5},{7,6},{8,7},{9,8},{10,9},{11,1... | collective-permute-start | bytes 49160 | tf_op jit(solution)/shard_map/ppermute | solution.py:27
  80.2 13.3 %collective-permute-start.6 = (f32[1,32,128]{2,1,0:T(8,128)S(1)}, f32[1,32,128]{2,1,0:T(8,128)S(1)}, u32[]{:S(2)}, u32[]{:S(2)}) collective-permute-start(f32[1,32,128]{2,1,0:T(8,128)S(1)} %get-tuple-element.151), channel_id=1, source_target_pairs={{0,1},{1,2},{2,3},{3,4},{4,5},{5,6},{6,7},{7,8},{8,9},{9,10},{10,1... | collective-permute-start | bytes 49160 | tf_op jit(solution)/shard_map/ppermute | solution.py:25
  86.4 7.3 collective-permute-start.14
  88.3 6.0 collective-permute-start.15
  93.7 1.1 copy-start.44
  94.8 8.0 %copy-start.56 = (s32[1,128]{1,0:T(1,128)S(1)}, s32[1,128]{1,0:T(1,128)}, u32[]{:S(2)}) copy-start(s32[1,128]{1,0:T(1,128)} %param.30) | copy-start | bytes 1540
  95.1 8.4 %collective-permute-start.8 = (f32[1,32,128]{2,1,0:T(8,128)S(1)}, f32[1,32,128]{2,1,0:T(8,128)S(1)}, u32[]{:S(2)}, u32[]{:S(2)}) collective-permute-start(f32[1,32,128]{2,1,0:T(8,128)S(1)} %get-tuple-element.148), channel_id=1, source_target_pairs={{1,0},{2,1},{3,2},{4,3},{5,4},{6,5},{7,6},{8,7},{9,8},{10,9},{11,1... | collective-permute-start | bytes 49160 | tf_op jit(solution)/shard_map/ppermute | solution.py:27
  97.1 6.6 collective-permute-start.9
  104.2 10.6 %collective-permute-start.10 = (f32[1,32,128]{2,1,0:T(8,128)S(1)}, f32[1,32,128]{2,1,0:T(8,128)S(1)}, u32[]{:S(2)}, u32[]{:S(2)}) collective-permute-start(f32[1,32,128]{2,1,0:T(8,128)S(1)} %get-tuple-element.146), channel_id=1, source_target_pairs={{1,0},{2,1},{3,2},{4,3},{5,4},{6,5},{7,6},{8,7},{9,8},{10,9},{11,1... | collective-permute-start | bytes 49160 | tf_op jit(solution)/shard_map/ppermute | solution.py:27
  106.1 8.7 %collective-permute-start.11 = (f32[1,32,128]{2,1,0:T(8,128)S(1)}, f32[1,32,128]{2,1,0:T(8,128)S(1)}, u32[]{:S(2)}, u32[]{:S(2)}) collective-permute-start(f32[1,32,128]{2,1,0:T(8,128)S(1)} %get-tuple-element.145), channel_id=1, source_target_pairs={{0,1},{1,2},{2,3},{3,4},{4,5},{5,6},{6,7},{7,8},{8,9},{9,10},{10,1... | collective-permute-start | bytes 49160 | tf_op jit(solution)/shard_map/ppermute | solution.py:25
  115.0 1.5 copy-start.54
  118.0 14.2 %collective-permute-start.16 = (f32[1,32,128]{2,1,0:T(8,128)S(1)}, f32[1,32,128]{2,1,0:T(8,128)S(1)}, u32[]{:S(2)}, u32[]{:S(2)}) collective-permute-start(f32[1,32,128]{2,1,0:T(8,128)S(1)} %get-tuple-element.142), channel_id=1, source_target_pairs={{1,0},{2,1},{3,2},{4,3},{5,4},{6,5},{7,6},{8,7},{9,8},{10,9},{11,1... | collective-permute-start | bytes 49160 | tf_op jit(solution)/shard_map/ppermute | solution.py:27
  120.0 12.3 %collective-permute-start.17 = (f32[1,32,128]{2,1,0:T(8,128)S(1)}, f32[1,32,128]{2,1,0:T(8,128)S(1)}, u32[]{:S(2)}, u32[]{:S(2)}) collective-permute-start(f32[1,32,128]{2,1,0:T(8,128)S(1)} %get-tuple-element.141), channel_id=1, source_target_pairs={{0,1},{1,2},{2,3},{3,4},{4,5},{5,6},{6,7},{7,8},{8,9},{9,10},{10,1... | collective-permute-start | bytes 49160 | tf_op jit(solution)/shard_map/ppermute | solution.py:25
  125.1 16.4 %collective-permute-start.12 = (f32[1,32,128]{2,1,0:T(8,128)S(1)}, f32[1,32,128]{2,1,0:T(8,128)S(1)}, u32[]{:S(2)}, u32[]{:S(2)}) collective-permute-start(f32[1,32,128]{2,1,0:T(8,128)S(1)} %get-tuple-element.144), channel_id=1, source_target_pairs={{1,0},{2,1},{3,2},{4,3},{5,4},{6,5},{7,6},{8,7},{9,8},{10,9},{11,1... | collective-permute-start | bytes 49160 | tf_op jit(solution)/shard_map/ppermute | solution.py:27
  127.0 14.5 %collective-permute-start.13 = (f32[1,32,128]{2,1,0:T(8,128)S(1)}, f32[1,32,128]{2,1,0:T(8,128)S(1)}, u32[]{:S(2)}, u32[]{:S(2)}) collective-permute-start(f32[1,32,128]{2,1,0:T(8,128)S(1)} %get-tuple-element.143), channel_id=1, source_target_pairs={{0,1},{1,2},{2,3},{3,4},{4,5},{5,6},{6,7},{7,8},{8,9},{9,10},{10,1... | collective-permute-start | bytes 49160 | tf_op jit(solution)/shard_map/ppermute | solution.py:25
  134.1 7.6 %collective-permute-start.18 = (f32[1,32,128]{2,1,0:T(8,128)S(1)}, f32[1,32,128]{2,1,0:T(8,128)S(1)}, u32[]{:S(2)}, u32[]{:S(2)}) collective-permute-start(f32[1,32,128]{2,1,0:T(8,128)S(1)} %get-tuple-element.140), channel_id=1, source_target_pairs={{1,0},{2,1},{3,2},{4,3},{5,4},{6,5},{7,6},{8,7},{9,8},{10,9},{11,1... | collective-permute-start | bytes 49160 | tf_op jit(solution)/shard_map/ppermute | solution.py:27
  136.0 6.4 collective-permute-start.19
  145.2 296.5 %all-reduce.17.cloned.1.call-start = ((), (), s32[]{:S(2)}) async-start(), calls=%async_computation | async-start | bytes 1769472 | tf_op jit(solution)/shard_map/psum | solution.py:13
  284.4 1.7 copy-start.25
  284.4 1.7 copy-start.27
  284.4 1.7 copy-start.39
  286.1 1.1 copy-start.37
  287.2 1.0 copy-start.19
  287.2 1.1 copy-start.35
  288.4 1.1 copy-start.33
  289.5 1.0 copy-start.11
  289.5 1.1 copy-start.31
  291.9 5.0 collective-permute-start.20
  293.7 5.4 collective-permute-start.21
  296.9 20.5 %copy-start.42 = (bf16[6,2,64,128]{3,2,1,0:T(8,128)(2,1)S(1)}, bf16[6,2,64,128]{3,2,1,0:T(8,128)(2,1)}, u32[]{:S(2)}) copy-start(bf16[6,2,64,128]{3,2,1,0:T(8,128)(2,1)} %copy-done.41) | copy-start | bytes 589828
  296.9 423.8 %all-reduce.19.cloned.1.call-start = ((), (), s32[]{:S(2)}) async-start(), calls=%async_computation.1 | async-start | bytes 1769472 | tf_op jit(solution)/shard_map/psum | solution.py:13
  299.0 117.0 %collective-permute-start.22 = (bf16[1,4,64,128]{3,2,1,0:T(8,128)(2,1)S(1)}, bf16[1,4,64,128]{3,2,1,0:T(8,128)(2,1)S(1)}, u32[]{:S(2)}, u32[]{:S(2)}) collective-permute-start(bf16[1,4,64,128]{3,2,1,0:T(8,128)(2,1)S(1)} %get-tuple-element.131), channel_id=1, source_target_pairs={{0,1},{1,2},{2,3},{3,4},{4,5},{5,6},{6,7},{7,8},{8,9},{9,10},{10,1... | collective-permute-start | bytes 196616 | tf_op jit(solution)/shard_map/ppermute | solution.py:25
  315.5 100.6 %collective-permute-start.23 = (bf16[1,4,64,128]{3,2,1,0:T(8,128)(2,1)S(1)}, bf16[1,4,64,128]{3,2,1,0:T(8,128)(2,1)S(1)}, u32[]{:S(2)}, u32[]{:S(2)}) collective-permute-start(bf16[1,4,64,128]{3,2,1,0:T(8,128)(2,1)S(1)} %get-tuple-element.132), channel_id=1, source_target_pairs={{1,0},{2,1},{3,2},{4,3},{5,4},{6,5},{7,6},{8,7},{9,8},{10,9},{11,1... | collective-permute-start | bytes 196616 | tf_op jit(solution)/shard_map/ppermute | solution.py:27
  421.3 20.5 %copy-start.46 = (bf16[1,1,3,64,64]{4,3,2,1,0:T(8,128)(2,1)S(1)}, bf16[1,1,3,64,64]{4,3,2,1,0:T(8,128)(2,1)}, u32[]{:S(2)}) copy-start(bf16[1,1,3,64,64]{4,3,2,1,0:T(8,128)(2,1)} %get-tuple-element.122) | copy-start | bytes 73732
  (21 other events, 18.2 us)
Sparse Core Ops, SparseCore 0:
  145.3 138.1 all-reduce.20
  297.1 144.6 all-reduce.16
  444.7 276.0 all-reduce.18
